TPU v7x, 256 devices: a whole 4x4x8 slice. The times are simulated.
256 devices in a mesh: band: 8 (over x, core), dom: 32 (over z, y).
Axes of the slice: x: 4, y: 4, z: 8, core: 2. Of those that a mesh axis runs over, the one named last changes fastest.
Arguments:
- orbitals: bfloat16 [256, 192, 48, 64], P('band', 'dom'), may hold values from -1.796875 to 1.796875
- potential: float32 [192, 48, 64], P('dom'), may hold values from -2 to 1
- projectors: float32 [2048, 128], P('dom'), may hold values from -1.5 to 1.5
- coupling: float32 [1024], P('dom'), may hold values from 0.5 to 2
- slot_block: int32 [2048], P('dom'), may hold values from 0 to 143
- slot_projector: int32 [2048], P('dom'), may hold values from 0 to 1023, as said below
- slot_count: int32 [32], P('dom'), may hold values from 16 to 64, as said below
- locked: bfloat16 [2048, 192, 3072], P(None, 'dom', 'band'), may hold values from -0.0078125 to 0.0078125
Outputs:
- orthogonal: bfloat16 [256, 192, 3072], P(None, 'dom', 'band')
- margins: float32 [2048, 256], P(('band', 'dom'))
Inputs may be any that keep to these rules, and one draw needn't show every extreme that they name: `slot_projector`: projector p belongs to domain p // 32; a slot of domain d names a projector of domain d - 1, d or d + 1, cyclically; slot 0 of every domain names one of domain d - 1 and slot 1 one of domain d + 1. The used slots of a domain are its first slot_count slots; some domain uses all and some uses 64 // 4.
All inputs are finite; a program needn't handle non-finite values.
Results may differ from a plain program's by a relative error of at most 0.0039.
The roundings to bfloat16 on the way count: a program that leaves them out, or rounds other values in their place, can miss the bound.
Values may be sent and summed in bfloat16 or wider, within the bound.
No kernel may reach another device: no remote copies, remote signals or barrier semaphores. Data moves between devices by JAX's collectives and lax.ppermute only.
A program may use at most 320 MiB of HBM per device.

v0:
```python
import jax
import jax.numpy as jnp
from jax import lax
from jax.sharding import PartitionSpec as P

BS = 128
PROJ_DOM = 32
COEFFS = (
    -5369.0 / 1800.0,
    12.0 / 7.0,
    -15.0 / 56.0,
    10.0 / 189.0,
    -1.0 / 112.0,
    2.0 / 825.0,
    -1.0 / 5544.0,
)


def with_halo(shard, sides, width):
    for axis, dim in sides:
        size, length = (lax.axis_size(axis), shard.shape[dim])
        up = [(i, (i + 1) % size) for i in range(size)]
        down = [(j, i) for i, j in up]
        last = lax.slice_in_dim(shard, length - width, length, axis=dim)
        initial = lax.slice_in_dim(shard, 0, width, axis=dim)
        before = lax.ppermute(last, axis, up)
        after = lax.ppermute(initial, axis, down)
        shard = jnp.concatenate([before, shard, after], axis=dim)
    return shard


def laplacian(orbital, extended):
    planes_x = orbital.shape[1]
    depth_z = orbital.shape[2]
    laplace = 3.0 * COEFFS[0] * orbital
    padded = jnp.pad(orbital, ((0, 0), (0, 0), (6, 6), (0, 0)))
    for offset in range(1, 7):
        weight = COEFFS[offset]
        laplace = laplace + weight * (
            extended[:, 6 + offset : 6 + offset + planes_x]
            + extended[:, 6 - offset : 6 - offset + planes_x]
        )
        laplace = laplace + weight * (jnp.roll(orbital, offset, 3) + jnp.roll(orbital, -offset, 3))
        laplace = laplace + weight * (
            padded[:, :, 6 + offset : 6 + offset + depth_z]
            + padded[:, :, 6 - offset : 6 - offset + depth_z]
        )
    return laplace


def per_device(
    orbitals, potential, projectors, coupling, slot_block, slot_projector, slot_count, locked
):
    orbital = orbitals.astype(jnp.float32)
    extended = with_halo(orbitals, (("dom", 1),), 6).astype(jnp.float32)
    laplace = laplacian(orbital, extended)
    band_rows, planes_x, depth_z, width_y = orbital.shape
    blocks_count = planes_x * depth_z * width_y // BS
    flat = orbital.reshape(band_rows, blocks_count, BS)
    blocks = flat[:, slot_block]
    slots = slot_block.shape[0]
    active = (jnp.arange(slots, dtype=jnp.int32) < slot_count[0]).astype(jnp.float32)
    inner_part = jnp.sum(blocks * projectors[None], axis=2) * active[None]
    domains = lax.axis_size("dom")
    here = lax.axis_index("dom")
    owner = slot_projector // PROJ_DOM
    local_id = slot_projector % PROJ_DOM
    relative = (owner - here + domains) % domains
    column = jnp.where(
        relative == 0,
        PROJ_DOM + local_id,
        jnp.where(relative == 1, 2 * PROJ_DOM + local_id, local_id),
    )
    onehot = (column[:, None] == jnp.arange(3 * PROJ_DOM, dtype=jnp.int32)[None, :]).astype(
        jnp.float32
    )
    partial_value = jnp.dot(inner_part, onehot, precision=lax.Precision.HIGHEST)
    outgoing = jnp.concatenate(
        [partial_value[:, :PROJ_DOM], partial_value[:, 2 * PROJ_DOM :]], axis=1
    )
    arrived = with_halo(outgoing, (("dom", 1),), PROJ_DOM)
    owned = (
        partial_value[:, PROJ_DOM : 2 * PROJ_DOM] + arrived[:, :PROJ_DOM] + arrived[:, -PROJ_DOM:]
    )
    table_local = owned * coupling[None]
    table = with_halo(table_local, (("dom", 1),), PROJ_DOM)
    slot_value = jnp.dot(table, onehot.T, precision=lax.Precision.HIGHEST) * active[None]
    contribution = slot_value[:, :, None] * projectors[None]
    nonlocal_term = jnp.zeros_like(flat).at[:, slot_block].add(contribution).reshape(orbital.shape)
    hamilton = -0.5 * laplace + potential[None] * orbital + nonlocal_term
    numerator, denominator = lax.psum(
        (jnp.sum(orbital * hamilton, axis=(1, 2, 3)), jnp.sum(orbital * orbital, axis=(1, 2, 3))),
        "dom",
    )
    energy = numerator / denominator
    residual = (hamilton - energy[:, None, None, None] * orbital).astype(jnp.bfloat16)
    residual = residual.reshape(band_rows, planes_x, depth_z * width_y)
    moved = lax.all_to_all(residual, "band", split_axis=2, concat_axis=0, tiled=True)
    all_bands = moved.shape[0]
    locked_flat = locked.reshape(locked.shape[0], -1)
    residual_flat = moved.reshape(all_bands, -1)
    contract_cells = (((1,), (1,)), ((), ()))
    share_rows = locked.shape[0] // lax.axis_size(("band", "dom"))
    summed = lax.psum(
        lax.dot_general(
            locked_flat, residual_flat, contract_cells, preferred_element_type=jnp.float32
        ),
        ("band", "dom"),
    )
    margins = lax.dynamic_slice_in_dim(
        summed, lax.axis_index(("band", "dom")) * share_rows, share_rows, 0
    )
    coeffs = summed.astype(jnp.bfloat16)
    correction = lax.dot_general(
        coeffs, locked_flat, (((0,), (0,)), ((), ())), preferred_element_type=jnp.float32
    )
    orthogonal = (
        (residual_flat.astype(jnp.float32) - correction).astype(jnp.bfloat16).reshape(moved.shape)
    )
    return (orthogonal, margins)


def solution(mesh):
    in_specs = (
        P("band", "dom", None, None),
        P("dom", None, None),
        P("dom", None),
        P("dom"),
        P("dom"),
        P("dom"),
        P("dom"),
        P(None, "dom", "band"),
    )
    out_specs = (P(None, "dom", "band"), P(("band", "dom"), None))
    return jax.shard_map(
        per_device, mesh=mesh, in_specs=in_specs, out_specs=out_specs, check_vma=False
    )
```

profile of v0, /device:TPU:2, one launch (start us, length us, event | category | flops | bytes accessed | tf_op | source)
XLA Modules:
  0.0 610.1 jit_solution(6926809845291708726)
XLA Ops:
  7.2 1.7 collective-permute-start
  8.8 6.8 %collective-permute-start.1 = (bf16[32,6,48,64]{3,2,1,0:T(8,128)(2,1)}, bf16[32,6,48,64]{3,2,1,0:T(8,128)(2,1)}, u32[]{:S(2)}, u32[]{:S(2)}) collective-permute-start(bf16[32,6,48,64]{3,2,1,0:T(8,128)(2,1)} %param.8), channel_id=1, source_target_pairs={{1,0},{2,1},{3,2},{4,3},{5,4},{6,5},{7,6},{8,7},{9,8},{10,9},{11,1... | collective-permute-start | bytes 3538952 | tf_op jit(solution)/shard_map/ppermute | solution.py:27
  15.7 4.4 reshape.34
  20.1 4.0 copy.30
  24.7 2.3 gather_fusion
  27.0 0.3 multiply_reduce_fusion
  27.4 0.3 fusion.50
  27.8 5.8 collective-permute-start.3
  33.5 4.6 fusion.65
  38.1 4.7 fusion.66
  42.8 4.7 fusion.67
  47.5 4.6 fusion.68
  52.1 4.6 fusion.69
  56.8 4.6 fusion.70
  61.3 4.7 fusion.71
  66.0 4.6 fusion.72
  70.6 4.6 fusion.73
  75.2 4.7 fusion.74
  79.9 4.6 fusion.75
  84.7 5.5 collective-permute-start.5
  90.2 4.7 fusion.76
  94.9 2.7 convert_element_type.28
  97.6 0.2 convolution_multiply_fusion
  97.7 0.1 copy.31
  97.9 0.3 multiply_bitcast_fusion
  98.2 1.7 broadcast_in_dim.4
  99.9 8.0 %scatter_fusion = f32[32,144,128]{2,0,1:T(8,128)} fusion(f32[32,144,128]{2,0,1:T(8,128)} %broadcast_in_dim.4, s32[64]{0:T(128)S(1)} %compare_select_fusion, f32[64,32,128]{2,1,0:T(8,128)S(1)} %multiply_bitcast_fusion), kind=kCustom, calls=%fused_computation.1 | custom fusion | flops 262144 | bytes 3145984 | tf_op jit(solution)/shard_map/scatter-add | solution.py:89
  108.0 4.5 copy.32
  112.4 4.5 reshape.35
  117.0 8.1 %maximum_convert_fusion = f32[32,18,48,64]{3,2,1,0:T(8,128)} fusion(bf16[32,6,48,64]{3,2,1,0:T(8,128)(2,1)} %collective-permute-done.1, bf16[32,6,48,64]{3,2,1,0:T(8,128)(2,1)S(1)} %copy-done, bf16[32,6,48,64]{3,2,1,0:T(8,128)(2,1)} %collective-permute-done), kind=kLoop, calls=%fused_computation.14 | loop fusion | flops 5308416 | bytes 10616832 | tf_op jit(solution)/shard_map/convert_element_type | solution.py:55
  125.1 75.7 %fusion.21 = (f32[32]{0:T(128)S(1)}, f32[32]{0:T(128)S(1)}, f32[32,6,48,64]{3,2,1,0:T(8,128)}) fusion(bf16[32,6,48,64]{3,2,1,0:T(8,128)(2,1)S(1)} %copy-done, f32[32,6,48,64]{3,2,1,0:T(8,128)} %reshape.35, f32[6,48,64]{2,1,0:T(8,128)S(1)} %copy-done.1, f32[32,6,48,6]{3,2,1,0:T(8,128)} %get-tuple-element.36, f32[32,6,48,58]{3,2,1,0:T(8,128)} %get-tuple-element.38, ...), kind=kLoop, calls=%fused_computation.41 | loop fusion | flops 44826560 | bytes 64954624 | tf_op jit(solution)/shard_map/reduce_sum | solution.py:92
  200.8 69.9 %all-reduce.1 = (f32[32]{0:T(128)S(1)}, f32[32]{0:T(128)S(1)}) all-reduce(f32[32]{0:T(128)S(1)} %get-tuple-element.11, f32[32]{0:T(128)S(1)} %get-tuple-element.10), channel_id=1, replica_groups=mesh['band'=8,'dom'=32] {'dom'}, use_global_device_ids=true, to_apply=%region_3.4 | all-reduce | flops 64 | bytes 512 | tf_op jit(solution)/shard_map/psum | solution.py:91
  270.7 4.6 fusion.23
  275.2 7.8 %copy.45 = bf16[32,6,48,64]{0,1,3,2:T(8,128)(2,1)} copy(bf16[32,6,48,64]{3,2,1,0:T(8,128)(2,1)} %fusion.23) | data formatting | bytes 2359296 | tf_op jit(solution)/shard_map/reshape | solution.py:97
  283.0 8.6 %reshape.59 = bf16[8,2,36864]{2,1,0:T(2,128)(2,1)} reshape(bf16[3072,6,32]{2,1,0:T(8,128)(2,1)} %bitcast.23) | data formatting | bytes 2359296
  291.6 4.8 all-to-all-start
  296.5 12.5 %copy.37 = bf16[2048,6,384]{0,2,1:T(8,128)(2,1)} copy(bf16[2048,6,384]{2,0,1:T(8,128)(2,1)} %param.15) | data formatting | bytes 18874368 | tf_op args[7]
  309.0 3.4 all-to-all-done
  312.4 6.2 %reshape.60 = bf16[3072,6,32]{2,1,0:T(8,128)(2,1)} reshape(bf16[8,2,36864]{2,1,0:T(2,128)(2,1)S(1)} %all-to-all-done) | data formatting | bytes 2359296
  318.5 6.5 %copy.36 = bf16[8,32,6,384]{3,2,1,0:T(8,128)(2,1)S(1)} copy(bf16[8,32,6,384]{1,2,3,0:T(8,128)(2,1)} %bitcast.24) | data formatting | bytes 2359296 | tf_op jit(solution)/shard_map/all_to_all | solution.py:98
  325.1 0.2 copy.46
  325.2 7.7 %convolution_bitcast_fusion = f32[2048,256]{0,1:T(8,128)} fusion(bf16[256,2304]{1,0:T(8,128)(2,1)S(1)} %bitcast.29, bf16[2048,2304]{0,1:T(8,128)(2,1)} %bitcast.25), kind=kOutput, calls=%fused_computation.82 | convolution fusion | flops 2415919104 | bytes 12713984 | tf_op jit(solution)/shard_map/dot_general | solution.py:105
  333.0 259.3 %all-reduce.4.cloned.1.call-done = f32[2048,256]{0,1:T(8,128)} async-done(((f32[2048,256]{0,1:T(8,128)}), f32[2048,256]{0,1:T(8,128)}) %all-reduce.4.cloned.1.call-update) | async-done | bytes 2097168 | tf_op jit(solution)/shard_map/psum | solution.py:104
  592.3 7.0 %fusion.48 = bf16[256,2304]{1,0:T(8,128)(2,1)S(1)} fusion(bf16[2048,2304]{0,1:T(8,128)(2,1)} %bitcast.26, bf16[256,2304]{1,0:T(8,128)(2,1)S(1)} %bitcast.30, f32[2048,256]{0,1:T(8,128)} %all-reduce.4.cloned.1.call-done), kind=kOutput, calls=%fused_computation.81 | convolution fusion | flops 2418212864 | bytes 13893632 | tf_op jit(solution)/shard_map/dot_general | solution.py:114
  599.3 0.6 copy.38
  599.9 1.4 copy.39
  601.4 1.0 constant_dynamic-slice_fusion
  602.4 0.7 copy.40
  (29 shorter events, 0.3 us)
Async XLA Ops:
  7.2 12.9 %copy-start.4 = (s32[64]{0:T(128)S(1)}, s32[64]{0:T(128)}, u32[]{:S(2)}) copy-start(s32[64]{0:T(128)} %param.12) | copy-start | bytes 772
  7.2 109.8 %collective-permute-start = (bf16[32,6,48,64]{3,2,1,0:T(8,128)(2,1)}, bf16[32,6,48,64]{3,2,1,0:T(8,128)(2,1)}, u32[]{:S(2)}, u32[]{:S(2)}) collective-permute-start(bf16[32,6,48,64]{3,2,1,0:T(8,128)(2,1)} %param.8), channel_id=1, source_target_pairs={{0,1},{1,2},{2,3},{3,4},{4,5},{5,6},{6,7},{7,8},{8,9},{9,10},{10,1... | collective-permute-start | bytes 3538952 | tf_op jit(solution)/shard_map/ppermute | solution.py:26
  8.8 108.2 %collective-permute-start.1 = (bf16[32,6,48,64]{3,2,1,0:T(8,128)(2,1)}, bf16[32,6,48,64]{3,2,1,0:T(8,128)(2,1)}, u32[]{:S(2)}, u32[]{:S(2)}) collective-permute-start(bf16[32,6,48,64]{3,2,1,0:T(8,128)(2,1)} %param.8), channel_id=1, source_target_pairs={{1,0},{2,1},{3,2},{4,3},{5,4},{6,5},{7,6},{8,7},{9,8},{10,9},{11,1... | collective-permute-start | bytes 3538952 | tf_op jit(solution)/shard_map/ppermute | solution.py:27
  15.7 9.1 %copy-start.5 = (s32[64]{0:T(128)S(1)}, s32[64]{0:T(128)}, u32[]{:S(2)}) copy-start(s32[64]{0:T(128)} %param.13) | copy-start | bytes 772
  15.7 11.4 %copy-start.2 = (f32[64,128]{1,0:T(8,128)S(1)}, f32[64,128]{1,0:T(8,128)}, u32[]{:S(2)}) copy-start(f32[64,128]{1,0:T(8,128)} %param.10) | copy-start | bytes 98308
  20.0 13.5 %copy-start = (bf16[32,6,48,64]{3,2,1,0:T(8,128)(2,1)S(1)}, bf16[32,6,48,64]{3,2,1,0:T(8,128)(2,1)}, u32[]{:S(2)}) copy-start(bf16[32,6,48,64]{3,2,1,0:T(8,128)(2,1)} %param.8) | copy-start | bytes 3538948
  27.7 56.8 %collective-permute-start.2 = (f32[32,32]{1,0:T(8,128)S(1)}, f32[32,32]{1,0:T(8,128)S(1)}, u32[]{:S(2)}, u32[]{:S(2)}) collective-permute-start(f32[32,32]{1,0:T(8,128)S(1)} %get-tuple-element.39), channel_id=1, source_target_pairs={{0,1},{1,2},{2,3},{3,4},{4,5},{5,6},{6,7},{7,8},{8,9},{9,10},{10,1... | collective-permute-start | bytes 12296 | tf_op jit(solution)/shard_map/ppermute | solution.py:26
  27.8 56.8 %collective-permute-start.3 = (f32[32,32]{1,0:T(8,128)S(1)}, f32[32,32]{1,0:T(8,128)S(1)}, u32[]{:S(2)}, u32[]{:S(2)}) collective-permute-start(f32[32,32]{1,0:T(8,128)S(1)} %get-tuple-element.40), channel_id=1, source_target_pairs={{1,0},{2,1},{3,2},{4,3},{5,4},{6,5},{7,6},{8,7},{9,8},{10,9},{11,1... | collective-permute-start | bytes 12296 | tf_op jit(solution)/shard_map/ppermute | solution.py:27
  79.9 4.7 copy-start.3
  84.6 12.9 %collective-permute-start.4 = (f32[32,32]{1,0:T(8,128)S(1)}, f32[32,32]{1,0:T(8,128)S(1)}, u32[]{:S(2)}, u32[]{:S(2)}) collective-permute-start(f32[32,32]{1,0:T(8,128)S(1)} %fusion.53), channel_id=1, source_target_pairs={{0,1},{1,2},{2,3},{3,4},{4,5},{5,6},{6,7},{7,8},{8,9},{9,10},{10,1... | collective-permute-start | bytes 12296 | tf_op jit(solution)/shard_map/ppermute | solution.py:26
  84.7 12.9 %collective-permute-start.5 = (f32[32,32]{1,0:T(8,128)S(1)}, f32[32,32]{1,0:T(8,128)S(1)}, u32[]{:S(2)}, u32[]{:S(2)}) collective-permute-start(f32[32,32]{1,0:T(8,128)S(1)} %fusion.53), channel_id=1, source_target_pairs={{1,0},{2,1},{3,2},{4,3},{5,4},{6,5},{7,6},{8,7},{9,8},{10,9},{11,1... | collective-permute-start | bytes 12296 | tf_op jit(solution)/shard_map/ppermute | solution.py:27
  117.0 8.1 %copy-start.1 = (f32[6,48,64]{2,1,0:T(8,128)S(1)}, f32[6,48,64]{2,1,0:T(8,128)}, u32[]{:S(2)}) copy-start(f32[6,48,64]{2,1,0:T(8,128)} %param.9) | copy-start | bytes 221188
  291.6 20.7 %all-to-all-start = ((bf16[8,2,36864]{2,1,0:T(2,128)(2,1)}), bf16[8,2,36864]{2,1,0:T(2,128)(2,1)S(1)}, u32[]{:S(2)}, u32[]{:S(2)}) async-start(bf16[8,2,36864]{2,1,0:T(2,128)(2,1)} %reshape.59), calls=%async_computation | async-start | bytes 2359296 | tf_op jit(solution)/shard_map/all_to_all | solution.py:98
  296.5 295.9 %all-reduce.4.cloned.1.call-start = ((), (), s32[]{:S(2)}) async-start(), calls=%async_computation.1 | async-start | bytes 4194304 | tf_op jit(solution)/shard_map/psum | solution.py:104
Sparse Core Ops, SparseCore 0:
  333.1 259.1 all-reduce.3
where the time goes:
time: 616 us; the launch traced here: 610 us
  waiting for transfers between devices  263 us (43%)
  local copies, waits for them, and re-layouts  123 us (20%)
  other arithmetic  99.9 us (16%)
  blocking collectives  69.9 us (11%)
  starting transfers between devices  24.7 us (4%)
  matrix products  15.2 us (2%)
  between operations  15.1 us (2%)
    psum x1, waiting for transfers between devices, per_device(): lax.psum(lax.dot_general(locked_flat, residual_flat, contract_cells, pref...  259 us
    reduce_sum x1, other arithmetic, per_device(): jnp.sum(orbital * orbital, axis=(1, 2, 3))  75.7 us
    psum x1, blocking collectives, per_device(): lax.psum((jnp.sum(orbital * hamilton, axis=(1, 2, 3)), jnp.sum(orbital *...  69.9 us
    slice x12, local copies, waits for them, and re-layouts, laplacian(): jnp.roll(orbital, offset, 3) + jnp.roll(orbital, -offset, 3)  55.6 us
    unnamed x18, local copies, waits for them, and re-layouts  29.6 us
    ppermute x3, starting transfers between devices, with_halo(): after = lax.ppermute(initial, axis, down)  18.1 us
  transfers between devices with their start and end apart: 8, of which 2 were waited for; matrix products, arithmetic and copies ran while one was open for 17% of the time, Pallas kernels for 0%

commit v1 on v0

--- a/solution.py
+++ b/solution.py
@@ -102,10 +102,13 @@
     contract_cells = (((1,), (1,)), ((), ()))
     share_rows = locked.shape[0] // lax.axis_size(("band", "dom"))
     summed = lax.psum(
-        lax.dot_general(
-            locked_flat, residual_flat, contract_cells, preferred_element_type=jnp.float32
+        lax.psum(
+            lax.dot_general(
+                locked_flat, residual_flat, contract_cells, preferred_element_type=jnp.float32
+            ),
+            "band",
         ),
-        ("band", "dom"),
+        "dom",
     )
     margins = lax.dynamic_slice_in_dim(
         summed, lax.axis_index(("band", "dom")) * share_rows, share_rows, 0

time: 616 us -> 582 us (0.945)
  waiting for transfers between devices: 263 us -> 229 us
    psum x1, waiting for transfers between devices: 259 us -> 66.2 us  [per_device(): lax.psum(lax.dot_general(locked_flat, residual_flat, contract_cells, pref...]
    psum x0 -> x1, waiting for transfers between devices: none -> 160 us  [per_device(): lax.psum(lax.psum(lax.dot_general(locked_flat, residual_flat, contract_ce...]
  transfers between devices with their start and end apart: 8 -> 9, of which waited for: 2 -> 3; matrix products, arithmetic and copies ran while one was open for 17% -> 18% of each run, Pallas kernels for 0% -> 0%
where the time goes in v1:
time: 582 us; the launch traced here: 577 us
  waiting for transfers between devices  229 us (39%)
  local copies, waits for them, and re-layouts  123 us (21%)
  other arithmetic  99.9 us (17%)
  blocking collectives  69.9 us (12%)
  starting transfers between devices  24.7 us (4%)
  matrix products  15.2 us (3%)
  between operations  15.1 us (3%)
    psum x1, waiting for transfers between devices, per_device(): lax.psum(lax.psum(lax.dot_general(locked_flat, residual_flat, contract_ce...  160 us
    reduce_sum x1, other arithmetic, per_device(): jnp.sum(orbital * orbital, axis=(1, 2, 3))  75.7 us
    psum x1, blocking collectives, per_device(): lax.psum((jnp.sum(orbital * hamilton, axis=(1, 2, 3)), jnp.sum(orbital *...  69.9 us
    psum x1, waiting for transfers between devices, per_device(): lax.psum(lax.dot_general(locked_flat, residual_flat, contract_cells, pref...  66.2 us
    slice x12, local copies, waits for them, and re-layouts, laplacian(): jnp.roll(orbital, offset, 3) + jnp.roll(orbital, -offset, 3)  55.6 us
    unnamed x18, local copies, waits for them, and re-layouts  29.6 us
    ppermute x3, starting transfers between devices, with_halo(): after = lax.ppermute(initial, axis, down)  18.1 us
  transfers between devices with their start and end apart: 9, of which 3 were waited for; matrix products, arithmetic and copies ran while one was open for 18% of the time, Pallas kernels for 0%

profile of v1, /device:TPU:2, one launch (start us, length us, event | category | flops | bytes accessed | tf_op | source)
XLA Modules:
  0.0 576.9 jit_solution(3505558557735273261)
XLA Ops:
  7.2 1.7 collective-permute-start
  8.8 6.8 %collective-permute-start.1 = (bf16[32,6,48,64]{3,2,1,0:T(8,128)(2,1)}, bf16[32,6,48,64]{3,2,1,0:T(8,128)(2,1)}, u32[]{:S(2)}, u32[]{:S(2)}) collective-permute-start(bf16[32,6,48,64]{3,2,1,0:T(8,128)(2,1)} %param.8), channel_id=1, source_target_pairs={{1,0},{2,1},{3,2},{4,3},{5,4},{6,5},{7,6},{8,7},{9,8},{10,9},{11,1... | collective-permute-start | bytes 3538952 | tf_op jit(solution)/shard_map/ppermute | solution.py:27
  15.7 4.4 reshape.34
  20.1 4.0 copy.30
  24.7 2.3 gather_fusion
  27.0 0.3 multiply_reduce_fusion
  27.4 0.3 fusion.50
  27.8 5.8 %collective-permute-start.3 = (f32[32,32]{1,0:T(8,128)S(1)}, f32[32,32]{1,0:T(8,128)S(1)}, u32[]{:S(2)}, u32[]{:S(2)}) collective-permute-start(f32[32,32]{1,0:T(8,128)S(1)} %get-tuple-element.40), channel_id=1, source_target_pairs={{1,0},{2,1},{3,2},{4,3},{5,4},{6,5},{7,6},{8,7},{9,8},{10,9},{11,1... | collective-permute-start | bytes 12296 | tf_op jit(solution)/shard_map/ppermute | solution.py:27
  33.5 4.6 fusion.65
  38.1 4.7 fusion.66
  42.8 4.7 fusion.67
  47.5 4.6 fusion.68
  52.1 4.6 fusion.69
  56.8 4.6 fusion.70
  61.3 4.7 fusion.71
  66.0 4.6 fusion.72
  70.6 4.6 fusion.73
  75.2 4.7 fusion.74
  79.9 4.6 fusion.75
  84.7 5.5 collective-permute-start.5
  90.2 4.7 fusion.76
  94.9 2.7 convert_element_type.28
  97.6 0.2 convolution_multiply_fusion
  97.9 0.3 multiply_bitcast_fusion
  98.2 1.7 broadcast_in_dim.4
  99.9 8.0 %scatter_fusion = f32[32,144,128]{2,0,1:T(8,128)} fusion(f32[32,144,128]{2,0,1:T(8,128)} %broadcast_in_dim.4, s32[64]{0:T(128)S(1)} %compare_select_fusion, f32[64,32,128]{2,1,0:T(8,128)S(1)} %multiply_bitcast_fusion), kind=kCustom, calls=%fused_computation.1 | custom fusion | flops 262144 | bytes 3145984 | tf_op jit(solution)/shard_map/scatter-add | solution.py:89
  108.0 4.5 copy.32
  112.4 4.5 reshape.35
  117.0 8.1 %maximum_convert_fusion = f32[32,18,48,64]{3,2,1,0:T(8,128)} fusion(bf16[32,6,48,64]{3,2,1,0:T(8,128)(2,1)} %collective-permute-done.1, bf16[32,6,48,64]{3,2,1,0:T(8,128)(2,1)S(1)} %copy-done, bf16[32,6,48,64]{3,2,1,0:T(8,128)(2,1)} %collective-permute-done), kind=kLoop, calls=%fused_computation.14 | loop fusion | flops 5308416 | bytes 10616832 | tf_op jit(solution)/shard_map/convert_element_type | solution.py:55
  125.1 75.7 %fusion.21 = (f32[32]{0:T(128)S(1)}, f32[32]{0:T(128)S(1)}, f32[32,6,48,64]{3,2,1,0:T(8,128)}) fusion(bf16[32,6,48,64]{3,2,1,0:T(8,128)(2,1)S(1)} %copy-done, f32[32,6,48,64]{3,2,1,0:T(8,128)} %reshape.35, f32[6,48,64]{2,1,0:T(8,128)S(1)} %copy-done.1, f32[32,6,48,6]{3,2,1,0:T(8,128)} %get-tuple-element.36, f32[32,6,48,58]{3,2,1,0:T(8,128)} %get-tuple-element.38, ...), kind=kLoop, calls=%fused_computation.41 | loop fusion | flops 44826560 | bytes 64954624 | tf_op jit(solution)/shard_map/reduce_sum | solution.py:92
  200.8 69.9 %all-reduce.1 = (f32[32]{0:T(128)S(1)}, f32[32]{0:T(128)S(1)}) all-reduce(f32[32]{0:T(128)S(1)} %get-tuple-element.11, f32[32]{0:T(128)S(1)} %get-tuple-element.10), channel_id=1, replica_groups=mesh['band'=8,'dom'=32] {'dom'}, use_global_device_ids=true, to_apply=%region_3.4 | all-reduce | flops 64 | bytes 512 | tf_op jit(solution)/shard_map/psum | solution.py:91
  270.7 4.6 fusion.23
  275.2 7.8 %copy.45 = bf16[32,6,48,64]{0,1,3,2:T(8,128)(2,1)} copy(bf16[32,6,48,64]{3,2,1,0:T(8,128)(2,1)} %fusion.23) | data formatting | bytes 2359296 | tf_op jit(solution)/shard_map/reshape | solution.py:97
  283.0 8.6 %reshape.59 = bf16[8,2,36864]{2,1,0:T(2,128)(2,1)} reshape(bf16[3072,6,32]{2,1,0:T(8,128)(2,1)} %bitcast.23) | data formatting | bytes 2359296
  291.6 4.8 all-to-all-start
  296.5 12.5 %copy.37 = bf16[2048,6,384]{0,2,1:T(8,128)(2,1)} copy(bf16[2048,6,384]{2,0,1:T(8,128)(2,1)} %param.15) | data formatting | bytes 18874368 | tf_op args[7]
  309.0 3.4 all-to-all-done
  312.4 6.2 %reshape.60 = bf16[3072,6,32]{2,1,0:T(8,128)(2,1)} reshape(bf16[8,2,36864]{2,1,0:T(2,128)(2,1)S(1)} %all-to-all-done) | data formatting | bytes 2359296
  318.5 6.5 %copy.36 = bf16[8,32,6,384]{3,2,1,0:T(8,128)(2,1)S(1)} copy(bf16[8,32,6,384]{1,2,3,0:T(8,128)(2,1)} %bitcast.24) | data formatting | bytes 2359296 | tf_op jit(solution)/shard_map/all_to_all | solution.py:98
  325.1 0.2 copy.46
  325.2 7.7 %convolution_bitcast_fusion = f32[2048,256]{0,1:T(8,128)} fusion(bf16[256,2304]{1,0:T(8,128)(2,1)S(1)} %bitcast.29, bf16[2048,2304]{0,1:T(8,128)(2,1)} %bitcast.25), kind=kOutput, calls=%fused_computation.82 | convolution fusion | flops 2415919104 | bytes 12713984 | tf_op jit(solution)/shard_map/dot_general | solution.py:106
  333.1 66.2 %all-reduce.5.cloned.1.call-done = f32[2048,256]{0,1:T(8,128)} async-done(((f32[2048,256]{0,1:T(8,128)}), f32[2048,256]{0,1:T(8,128)}) %all-reduce.5.cloned.1.call-update) | async-done | bytes 2097168 | tf_op jit(solution)/shard_map/psum | solution.py:105
  399.3 159.8 %all-reduce.7.cloned.1.call-done = f32[2048,256]{0,1:T(8,128)} async-done(((f32[2048,256]{0,1:T(8,128)}), f32[2048,256]{0,1:T(8,128)}) %all-reduce.7.cloned.1.call-update) | async-done | bytes 2097168 | tf_op jit(solution)/shard_map/psum | solution.py:104
  559.1 7.0 %fusion.48 = bf16[256,2304]{1,0:T(8,128)(2,1)S(1)} fusion(bf16[2048,2304]{0,1:T(8,128)(2,1)} %bitcast.26, bf16[256,2304]{1,0:T(8,128)(2,1)S(1)} %bitcast.30, f32[2048,256]{0,1:T(8,128)} %all-reduce.7.cloned.1.call-done), kind=kOutput, calls=%fused_computation.81 | convolution fusion | flops 2418212864 | bytes 13893632 | tf_op jit(solution)/shard_map/dot_general | solution.py:117
  566.1 0.6 copy.38
  566.7 1.4 copy.39
  568.1 1.0 constant_dynamic-slice_fusion
  569.1 0.7 copy.40
  (32 shorter events, 0.5 us)
Async XLA Ops:
  7.2 12.9 %copy-start.4 = (s32[64]{0:T(128)S(1)}, s32[64]{0:T(128)}, u32[]{:S(2)}) copy-start(s32[64]{0:T(128)} %param.12) | copy-start | bytes 772
  7.2 109.8 %collective-permute-start = (bf16[32,6,48,64]{3,2,1,0:T(8,128)(2,1)}, bf16[32,6,48,64]{3,2,1,0:T(8,128)(2,1)}, u32[]{:S(2)}, u32[]{:S(2)}) collective-permute-start(bf16[32,6,48,64]{3,2,1,0:T(8,128)(2,1)} %param.8), channel_id=1, source_target_pairs={{0,1},{1,2},{2,3},{3,4},{4,5},{5,6},{6,7},{7,8},{8,9},{9,10},{10,1... | collective-permute-start | bytes 3538952 | tf_op jit(solution)/shard_map/ppermute | solution.py:26
  8.8 108.2 %collective-permute-start.1 = (bf16[32,6,48,64]{3,2,1,0:T(8,128)(2,1)}, bf16[32,6,48,64]{3,2,1,0:T(8,128)(2,1)}, u32[]{:S(2)}, u32[]{:S(2)}) collective-permute-start(bf16[32,6,48,64]{3,2,1,0:T(8,128)(2,1)} %param.8), channel_id=1, source_target_pairs={{1,0},{2,1},{3,2},{4,3},{5,4},{6,5},{7,6},{8,7},{9,8},{10,9},{11,1... | collective-permute-start | bytes 3538952 | tf_op jit(solution)/shard_map/ppermute | solution.py:27
  15.7 9.1 %copy-start.5 = (s32[64]{0:T(128)S(1)}, s32[64]{0:T(128)}, u32[]{:S(2)}) copy-start(s32[64]{0:T(128)} %param.13) | copy-start | bytes 772
  15.7 11.4 %copy-start.2 = (f32[64,128]{1,0:T(8,128)S(1)}, f32[64,128]{1,0:T(8,128)}, u32[]{:S(2)}) copy-start(f32[64,128]{1,0:T(8,128)} %param.10) | copy-start | bytes 98308
  20.0 13.5 %copy-start = (bf16[32,6,48,64]{3,2,1,0:T(8,128)(2,1)S(1)}, bf16[32,6,48,64]{3,2,1,0:T(8,128)(2,1)}, u32[]{:S(2)}) copy-start(bf16[32,6,48,64]{3,2,1,0:T(8,128)(2,1)} %param.8) | copy-start | bytes 3538948
  27.7 56.8 %collective-permute-start.2 = (f32[32,32]{1,0:T(8,128)S(1)}, f32[32,32]{1,0:T(8,128)S(1)}, u32[]{:S(2)}, u32[]{:S(2)}) collective-permute-start(f32[32,32]{1,0:T(8,128)S(1)} %get-tuple-element.39), channel_id=1, source_target_pairs={{0,1},{1,2},{2,3},{3,4},{4,5},{5,6},{6,7},{7,8},{8,9},{9,10},{10,1... | collective-permute-start | bytes 12296 | tf_op jit(solution)/shard_map/ppermute | solution.py:26
  27.8 56.8 %collective-permute-start.3 = (f32[32,32]{1,0:T(8,128)S(1)}, f32[32,32]{1,0:T(8,128)S(1)}, u32[]{:S(2)}, u32[]{:S(2)}) collective-permute-start(f32[32,32]{1,0:T(8,128)S(1)} %get-tuple-element.40), channel_id=1, source_target_pairs={{1,0},{2,1},{3,2},{4,3},{5,4},{6,5},{7,6},{8,7},{9,8},{10,9},{11,1... | collective-permute-start | bytes 12296 | tf_op jit(solution)/shard_map/ppermute | solution.py:27
  79.9 4.7 copy-start.3
  84.6 12.9 %collective-permute-start.4 = (f32[32,32]{1,0:T(8,128)S(1)}, f32[32,32]{1,0:T(8,128)S(1)}, u32[]{:S(2)}, u32[]{:S(2)}) collective-permute-start(f32[32,32]{1,0:T(8,128)S(1)} %fusion.53), channel_id=1, source_target_pairs={{0,1},{1,2},{2,3},{3,4},{4,5},{5,6},{6,7},{7,8},{8,9},{9,10},{10,1... | collective-permute-start | bytes 12296 | tf_op jit(solution)/shard_map/ppermute | solution.py:26
  84.7 12.9 %collective-permute-start.5 = (f32[32,32]{1,0:T(8,128)S(1)}, f32[32,32]{1,0:T(8,128)S(1)}, u32[]{:S(2)}, u32[]{:S(2)}) collective-permute-start(f32[32,32]{1,0:T(8,128)S(1)} %fusion.53), channel_id=1, source_target_pairs={{1,0},{2,1},{3,2},{4,3},{5,4},{6,5},{7,6},{8,7},{9,8},{10,9},{11,1... | collective-permute-start | bytes 12296 | tf_op jit(solution)/shard_map/ppermute | solution.py:27
  117.0 8.1 %copy-start.1 = (f32[6,48,64]{2,1,0:T(8,128)S(1)}, f32[6,48,64]{2,1,0:T(8,128)}, u32[]{:S(2)}) copy-start(f32[6,48,64]{2,1,0:T(8,128)} %param.9) | copy-start | bytes 221188
  291.6 20.7 %all-to-all-start = ((bf16[8,2,36864]{2,1,0:T(2,128)(2,1)}), bf16[8,2,36864]{2,1,0:T(2,128)(2,1)S(1)}, u32[]{:S(2)}, u32[]{:S(2)}) async-start(bf16[8,2,36864]{2,1,0:T(2,128)(2,1)} %reshape.59), calls=%async_computation | async-start | bytes 2359296 | tf_op jit(solution)/shard_map/all_to_all | solution.py:98
  296.5 102.8 %all-reduce.5.cloned.1.call-start = ((), (), s32[]{:S(2)}) async-start(), calls=%async_computation.1 | async-start | bytes 4194304 | tf_op jit(solution)/shard_map/psum | solution.py:105
  333.0 226.1 %all-reduce.7.cloned.1.call-start = ((), (), s32[]{:S(2)}) async-start(), calls=%async_computation.2 | async-start | bytes 4194304 | tf_op jit(solution)/shard_map/psum | solution.py:104
Sparse Core Ops, SparseCore 0:
  333.1 66.1 all-reduce.4
  402.8 156.2 all-reduce.6
